TPU v7x, 32 devices: a whole 2x2x4 slice. The times are simulated.
32 devices in a mesh: seq: 8 (over z, y), ch: 4 (over x, core).
Axes of the slice: x: 2, y: 2, z: 4, core: 2. Of those that a mesh axis runs over, the one named last changes fastest.
Arguments:
- stream: bfloat16 [2048, 1536], P('seq', 'ch'), may hold values from -6 to 6
- norm_gain: float32 [9, 1536], replicated, may hold values from 0.25 to 1.75
- conv_weight: bfloat16 [8, 3, 1536, 768], P(None, None, 'seq', 'ch'), may hold values from -0.09375 to 0.09375
- conv_bias: float32 [8, 768], P(None, 'ch'), may hold values from -3 to 3
- point_weight: bfloat16 [8, 768, 1536], P(None, 'seq', 'ch'), may hold values from -0.21875 to 0.21875
- point_bias: float32 [8, 1536], P(None, 'ch'), may hold values from -2 to 2
- head_weight: bfloat16 [1536, 3840], P('seq', 'ch'), may hold values from -0.15625 to 0.15625
- head_bias: float32 [3840], P('ch'), may hold values from -3 to 3
- exon_start: int32 [512], replicated, may hold values from 0 to 2016, as said below
- exon_length: int32 [512], replicated, may hold values from 1 to 32
- exon_transcript: int32 [512], replicated, may hold values from 0 to 63, as said below
- transcript_slot: int32 [64], replicated, may hold values from 0 to 63, each once
Outputs:
- transcript_cov: float32 [64, 3840], P('seq', 'ch')
Inputs may be any that keep to these rules, and one draw needn't show every extreme that they name: An exon of transcript t starts in bins t * 32 to t * 32 + 31, and exon_start[e] + exon_length[e] <= 2048. `exon_transcript`: never falls along the exons; every transcript has 1 to 15 exons, one exactly 15; transcripts 2 i and 2 i + 1 together have 2 * 8. `transcript_slot`: each row once.
All inputs are finite; a program needn't handle non-finite values.
Results may differ from a plain program's by a relative error of at most 0.00065.
Values may be sent and summed in bfloat16 or wider, within the bound.
A program may use at most 128 MiB of HBM per device.

v0:
```python
import jax
import jax.numpy as jnp
from jax import lax
from jax.sharding import PartitionSpec as P

LAYERS = 8


def padded(block, sides, width):
    for axis, dim in sides:
        count = lax.axis_size(axis)
        forward = [(i, i + 1) for i in range(count - 1)]
        backward = [(target, source) for source, target in forward]
        low = lax.ppermute(
            lax.slice_in_dim(block, block.shape[dim] - width, None, axis=dim), axis, forward
        )
        high = lax.ppermute(lax.slice_in_dim(block, 0, width, axis=dim), axis, backward)
        block = jnp.concatenate([low, block, high], axis=dim)
    return block


def rms_scaled(values, gain_row):
    wide = values.astype(jnp.float32)
    scale = lax.rsqrt(jnp.mean(wide * wide, axis=-1, keepdims=True) + 1e-06)
    return wide * scale * gain_row


def local(
    stream,
    norm_gain,
    conv_weight,
    conv_bias,
    point_weight,
    point_bias,
    head_weight,
    head_bias,
    exon_start,
    exon_length,
    exon_transcript,
    transcript_slot,
):
    bin_rows = stream.shape[0]
    resid = stream
    for layer_idx in range(LAYERS):
        spread = 2**layer_idx
        rimmed = padded(resid, (("seq", 0),), spread)
        full_rows = lax.all_gather(rimmed, "ch", axis=1, tiled=True)
        act_rows = jax.nn.gelu(
            rms_scaled(full_rows, norm_gain[layer_idx]), approximate=False
        ).astype(jnp.bfloat16)
        tap_rows = jnp.stack(
            [
                act_rows[0:bin_rows],
                act_rows[spread : spread + bin_rows],
                act_rows[2 * spread : 2 * spread + bin_rows],
            ]
        )
        conv_sum = jnp.einsum(
            "kbc,kch->bh",
            tap_rows,
            lax.all_gather(conv_weight[layer_idx], "seq", axis=1, tiled=True),
            preferred_element_type=jnp.float32,
        )
        hidden = jax.nn.gelu(conv_sum + conv_bias[layer_idx], approximate=False).astype(
            jnp.bfloat16
        )
        hidden_all = lax.all_gather(hidden, "ch", axis=1, tiled=True)
        mixed = jnp.dot(
            hidden_all,
            lax.all_gather(point_weight[layer_idx], "seq", axis=0, tiled=True),
            preferred_element_type=jnp.float32,
        )
        resid = (resid.astype(jnp.float32) + mixed + point_bias[layer_idx]).astype(jnp.bfloat16)
    final_all = lax.all_gather(resid, "ch", axis=1, tiled=True)
    final_rows = rms_scaled(final_all, norm_gain[LAYERS]).astype(jnp.bfloat16)
    logits = jnp.dot(
        final_rows,
        lax.all_gather(head_weight, "seq", axis=0, tiled=True),
        preferred_element_type=jnp.float32,
    )
    coverage = jax.nn.softplus(logits + head_bias)
    seq_index = lax.axis_index("seq")
    bin_ids = seq_index * bin_rows + jnp.arange(bin_rows, dtype=jnp.int32)
    member = (
        (bin_ids[None, :] >= exon_start[:, None])
        & (bin_ids[None, :] < (exon_start + exon_length)[:, None])
    ).astype(jnp.bfloat16)
    owner_rows = transcript_slot[exon_transcript]
    select = (
        owner_rows[None, :] == jnp.arange(transcript_slot.shape[0], dtype=jnp.int32)[:, None]
    ).astype(jnp.bfloat16)
    counts = jnp.dot(select, member, preferred_element_type=jnp.float32)
    total = lax.psum_scatter(
        jnp.dot(counts, coverage, precision=lax.Precision.HIGHEST),
        "seq",
        scatter_dimension=0,
        tiled=True,
    )
    return jnp.log1p(total)


def solution(mesh):
    placed = (
        P("seq", "ch"),
        P(),
        P(None, None, "seq", "ch"),
        P(None, "ch"),
        P(None, "seq", "ch"),
        P(None, "ch"),
        P("seq", "ch"),
        P("ch"),
        P(),
        P(),
        P(),
        P(),
    )
    return jax.shard_map(
        local, mesh=mesh, in_specs=placed, out_specs=P("seq", "ch"), check_vma=False
    )
```

profile of v0, /device:TPU:0, one launch (start us, length us, event | category | flops | bytes accessed | tf_op | source)
XLA Modules:
  0.0 757.6 jit_solution(6026623171330266288)
XLA Ops:
  24.3 35.3 %all-gather.1 = bf16[1,768,384]{2,1,0:T(8,128)(2,1)S(1)} all-gather(bf16[1,96,384]{2,1,0:T(8,128)(2,1)S(1)} %get-tuple-element.60), channel_id=3, replica_groups=mesh['seq'=8,'ch'=4] {'seq'}, dimensions={1}, use_global_device_ids=true | all-gather | bytes 663552 | tf_op jit(solution)/shard_map/all_gather | solution.py:70
  60.4 8.5 %all_gather.102 = bf16[258,1536]{1,0:T(8,128)(2,1)S(1)} all-gather(bf16[258,384]{1,0:T(8,128)(2,1)S(1)} %pad_maximum_fusion.5), channel_id=1, replica_groups=mesh['seq'=8,'ch'=4] {'ch'}, dimensions={1}, use_global_device_ids=true | all-gather | bytes 990720 | tf_op jit(solution)/shard_map/all_gather | solution.py:47
  95.4 34.9 %all-gather.3 = bf16[1,768,384]{2,1,0:T(8,128)(2,1)S(1)} all-gather(bf16[1,96,384]{2,1,0:T(8,128)(2,1)S(1)} %copy-done.9), channel_id=5, replica_groups=mesh['seq'=8,'ch'=4] {'seq'}, dimensions={1}, use_global_device_ids=true | all-gather | bytes 663552 | tf_op jit(solution)/shard_map/all_gather | solution.py:70
  130.4 16.3 %all-gather.36.cloned.1.call-done = bf16[1,3,1536,192]{3,1,0,2:T(4,128)(2,1)} async-done(((bf16[1,3,192,192]{3,1,0,2:T(4,128)(2,1)}), bf16[1,3,1536,192]{3,1,0,2:T(4,128)(2,1)}) %all-gather.36.cloned.1.call-update) | async-done | bytes 1769488 | tf_op jit(solution)/shard_map/all_gather | solution.py:61
  151.0 8.7 %all_gather.106 = bf16[260,1536]{1,0:T(8,128)(2,1)S(1)} all-gather(bf16[260,384]{1,0:T(8,128)(2,1)S(1)} %pad_maximum_fusion.6), channel_id=1, replica_groups=mesh['seq'=8,'ch'=4] {'ch'}, dimensions={1}, use_global_device_ids=true | all-gather | bytes 998400 | tf_op jit(solution)/shard_map/all_gather | solution.py:47
  176.3 35.1 %all-gather.5 = bf16[1,768,384]{2,1,0:T(8,128)(2,1)S(1)} all-gather(bf16[1,96,384]{2,1,0:T(8,128)(2,1)S(1)} %copy-done.8), channel_id=7, replica_groups=mesh['seq'=8,'ch'=4] {'seq'}, dimensions={1}, use_global_device_ids=true | all-gather | bytes 663552 | tf_op jit(solution)/shard_map/all_gather | solution.py:70
  211.4 7.3 all-gather.38.cloned.1.call-done
  223.0 9.1 %all_gather.110 = bf16[264,1536]{1,0:T(8,128)(2,1)S(1)} all-gather(bf16[264,384]{1,0:T(8,128)(2,1)S(1)} %pad_maximum_fusion.7), channel_id=1, replica_groups=mesh['seq'=8,'ch'=4] {'ch'}, dimensions={1}, use_global_device_ids=true | all-gather | bytes 1013760 | tf_op jit(solution)/shard_map/all_gather | solution.py:47
  249.3 34.3 %all-gather.7 = bf16[1,768,384]{2,1,0:T(8,128)(2,1)S(1)} all-gather(bf16[1,96,384]{2,1,0:T(8,128)(2,1)S(1)} %copy-done.7), channel_id=9, replica_groups=mesh['seq'=8,'ch'=4] {'seq'}, dimensions={1}, use_global_device_ids=true | all-gather | bytes 663552 | tf_op jit(solution)/shard_map/all_gather | solution.py:70
  283.5 7.8 %all-gather.40.cloned.1.call-done = bf16[1,3,1536,192]{3,1,0,2:T(4,128)(2,1)} async-done(((bf16[1,3,192,192]{3,1,0,2:T(4,128)(2,1)}), bf16[1,3,1536,192]{3,1,0,2:T(4,128)(2,1)}) %all-gather.40.cloned.1.call-update) | async-done | bytes 1769488 | tf_op jit(solution)/shard_map/all_gather | solution.py:61
  295.6 9.2 %all_gather.114 = bf16[272,1536]{1,0:T(8,128)(2,1)S(1)} all-gather(bf16[272,384]{1,0:T(8,128)(2,1)S(1)} %pad_maximum_fusion.4), channel_id=1, replica_groups=mesh['seq'=8,'ch'=4] {'ch'}, dimensions={1}, use_global_device_ids=true | all-gather | bytes 1044480 | tf_op jit(solution)/shard_map/all_gather | solution.py:47
  321.8 34.1 %all-gather.9 = bf16[1,768,384]{2,1,0:T(8,128)(2,1)S(1)} all-gather(bf16[1,96,384]{2,1,0:T(8,128)(2,1)S(1)} %copy-done.6), channel_id=11, replica_groups=mesh['seq'=8,'ch'=4] {'seq'}, dimensions={1}, use_global_device_ids=true | all-gather | bytes 663552 | tf_op jit(solution)/shard_map/all_gather | solution.py:70
  355.9 7.4 all-gather.42.cloned.1.call-done
  367.5 10.1 %all_gather.118 = bf16[288,1536]{1,0:T(8,128)(2,1)S(1)} all-gather(bf16[288,384]{1,0:T(8,128)(2,1)S(1)} %pad_maximum_fusion.3), channel_id=1, replica_groups=mesh['seq'=8,'ch'=4] {'ch'}, dimensions={1}, use_global_device_ids=true | all-gather | bytes 1105920 | tf_op jit(solution)/shard_map/all_gather | solution.py:47
  395.0 34.0 %all-gather.11 = bf16[1,768,384]{2,1,0:T(8,128)(2,1)S(1)} all-gather(bf16[1,96,384]{2,1,0:T(8,128)(2,1)S(1)} %copy-done.5), channel_id=13, replica_groups=mesh['seq'=8,'ch'=4] {'seq'}, dimensions={1}, use_global_device_ids=true | all-gather | bytes 663552 | tf_op jit(solution)/shard_map/all_gather | solution.py:70
  440.5 9.7 %all_gather.122 = bf16[320,1536]{1,0:T(8,128)(2,1)S(1)} all-gather(bf16[320,384]{1,0:T(8,128)(2,1)S(1)} %pad_maximum_fusion.2), channel_id=1, replica_groups=mesh['seq'=8,'ch'=4] {'ch'}, dimensions={1}, use_global_device_ids=true | all-gather | bytes 1228800 | tf_op jit(solution)/shard_map/all_gather | solution.py:47
  475.8 33.1 %all-gather.13 = bf16[1,768,384]{2,1,0:T(8,128)(2,1)S(1)} all-gather(bf16[1,96,384]{2,1,0:T(8,128)(2,1)S(1)} %copy-done.4), channel_id=15, replica_groups=mesh['seq'=8,'ch'=4] {'seq'}, dimensions={1}, use_global_device_ids=true | all-gather | bytes 663552 | tf_op jit(solution)/shard_map/all_gather | solution.py:70
  513.2 11.9 %all-gather.28.cloned.1.call-done = bf16[384,1536]{1,0:T(8,128)(2,1)} async-done(((bf16[384,384]{1,0:T(8,128)(2,1)}), bf16[384,1536]{1,0:T(8,128)(2,1)}) %all-gather.28.cloned.1.call-update) | async-done | bytes 1179664 | tf_op jit(solution)/shard_map/all_gather | solution.py:47
  555.8 34.5 %all-gather.15 = bf16[1,768,384]{2,1,0:T(8,128)(2,1)S(1)} all-gather(bf16[1,96,384]{2,1,0:T(8,128)(2,1)S(1)} %get-tuple-element.54), channel_id=17, replica_groups=mesh['seq'=8,'ch'=4] {'seq'}, dimensions={1}, use_global_device_ids=true | all-gather | bytes 663552 | tf_op jit(solution)/shard_map/all_gather | solution.py:70
  590.4 40.0 %select_select_fusion = s32[512]{0:T(512)S(1)} fusion(s32[512]{0:T(512)S(1)} %copy-done.29, s32[]{:T(128)} %bitcast, s32[]{:T(128)} %bitcast.1, s32[]{:T(128)} %bitcast.2, s32[]{:T(128)} %bitcast.3, s32[]{:T(128)} %bitcast.4, s32[]{:T(128)} %bitcast.5, s32[]{:T(128)} %bitcast.6, s32[]{:T(128)} %bitcast.7, s32[]{:T(128)} %bitcast.8, s32[]{:T(128)} %bitcast.9, ...), kind=kLoop, calls=%fused_computation.538 | loop fusion | flops 66048 | bytes 4352 | tf_op jit(solution)/shard_map/gather | solution.py:88
  636.9 7.5 fusion.5
  652.9 9.0 %all_gather.134 = bf16[256,1536]{1,0:T(8,128)(2,1)S(1)} all-gather(bf16[256,384]{1,0:T(8,128)(2,1)S(1)} %fusion.266), channel_id=1, replica_groups=mesh['seq'=8,'ch'=4] {'ch'}, dimensions={1}, use_global_device_ids=true | all-gather | bytes 983040 | tf_op jit(solution)/shard_map/all_gather | solution.py:74
  662.2 21.2 %all-gather.32.cloned.1.call-done = bf16[1536,960]{1,0:T(8,128)(2,1)} async-done(((bf16[192,960]{1,0:T(8,128)(2,1)}), bf16[1536,960]{1,0:T(8,128)(2,1)}) %all-gather.32.cloned.1.call-update) | async-done | bytes 2949136 | tf_op jit(solution)/shard_map/all_gather | solution.py:78
  688.8 60.0 %reduce-scatter.2.cloned.1.call-done = f32[8,960]{1,0:T(8,128)} async-done(((f32[64,960]{1,0:T(8,128)}), f32[8,960]{1,0:T(8,128)}) %reduce-scatter.2.cloned.1.call-update) | async-done | bytes 30736 | tf_op jit(solution)/shard_map/reduce_scatter | solution.py:93
  (243 shorter events, 223.3 us)
Async XLA Ops:
  6.5 71.1 %all-gather.34.cloned.1.call-start = ((), (), s32[]{:S(2)}) async-start(), calls=%async_computation.5 | async-start | bytes 3538944 | tf_op jit(solution)/shard_map/all_gather | solution.py:61
  9.3 137.3 %all-gather.36.cloned.1.call-start = ((), (), s32[]{:S(2)}) async-start(), calls=%async_computation.6 | async-start | bytes 3538944 | tf_op jit(solution)/shard_map/all_gather | solution.py:61
  10.4 208.3 %all-gather.38.cloned.1.call-start = ((), (), s32[]{:S(2)}) async-start(), calls=%async_computation.7 | async-start | bytes 3538944 | tf_op jit(solution)/shard_map/all_gather | solution.py:61
  11.5 279.8 %all-gather.40.cloned.1.call-start = ((), (), s32[]{:S(2)}) async-start(), calls=%async_computation.8 | async-start | bytes 3538944 | tf_op jit(solution)/shard_map/all_gather | solution.py:61
  12.6 350.6 %all-gather.42.cloned.1.call-start = ((), (), s32[]{:S(2)}) async-start(), calls=%async_computation.9 | async-start | bytes 3538944 | tf_op jit(solution)/shard_map/all_gather | solution.py:61
  13.8 422.5 %all-gather.44.cloned.1.call-start = ((), (), s32[]{:S(2)}) async-start(), calls=%async_computation.10 | async-start | bytes 3538944 | tf_op jit(solution)/shard_map/all_gather | solution.py:61
  14.8 494.1 %all-gather.46.cloned.1.call-start = ((), (), s32[]{:S(2)}) async-start(), calls=%async_computation.11 | async-start | bytes 3538944 | tf_op jit(solution)/shard_map/all_gather | solution.py:61
  14.9 45.4 %collective-permute-start = (bf16[1,384]{1,0:T(2,128)(2,1)S(1)}, bf16[1,384]{1,0:T(2,128)(2,1)S(1)}, u32[]{:S(2)}, u32[]{:S(2)}) collective-permute-start(bf16[1,384]{1,0:T(2,128)(2,1)S(1)} %get-tuple-element.76), channel_id=1, source_target_pairs={{0,4},{4,8},{8,12},{12,16},{16,20},{20,24},{24,28},{1,5},{5,9},{9,... | collective-permute-start | bytes 2312 | tf_op jit(solution)/shard_map/ppermute | solution.py:14
  19.8 40.5 %collective-permute-start.1 = (bf16[1,384]{1,0:T(2,128)(2,1)S(1)}, bf16[1,384]{1,0:T(2,128)(2,1)S(1)}, u32[]{:S(2)}, u32[]{:S(2)}) collective-permute-start(bf16[1,384]{1,0:T(2,128)(2,1)S(1)} %get-tuple-element.77), channel_id=1, source_target_pairs={{4,0},{8,4},{12,8},{16,12},{20,16},{24,20},{28,24},{5,1},{9,5},{13... | collective-permute-start | bytes 2312 | tf_op jit(solution)/shard_map/ppermute | solution.py:17
  22.1 502.9 %all-gather.28.cloned.1.call-start = ((), (), s32[]{:S(2)}) async-start(), calls=%async_computation.1 | async-start | bytes 1474560 | tf_op jit(solution)/shard_map/all_gather | solution.py:47
  91.6 59.3 %collective-permute-start.2 = (bf16[2,384]{1,0:T(2,128)(2,1)S(1)}, bf16[2,384]{1,0:T(2,128)(2,1)S(1)}, u32[]{:S(2)}, u32[]{:S(2)}) collective-permute-start(bf16[2,384]{1,0:T(2,128)(2,1)S(1)} %get-tuple-element.74), channel_id=1, source_target_pairs={{0,4},{4,8},{8,12},{12,16},{16,20},{20,24},{24,28},{1,5},{5,9},{9,... | collective-permute-start | bytes 4616 | tf_op jit(solution)/shard_map/ppermute | solution.py:14
  94.1 56.8 %collective-permute-start.3 = (bf16[2,384]{1,0:T(2,128)(2,1)S(1)}, bf16[2,384]{1,0:T(2,128)(2,1)S(1)}, u32[]{:S(2)}, u32[]{:S(2)}) collective-permute-start(bf16[2,384]{1,0:T(2,128)(2,1)S(1)} %get-tuple-element.75), channel_id=1, source_target_pairs={{4,0},{8,4},{12,8},{16,12},{20,16},{24,20},{28,24},{5,1},{9,5},{13... | collective-permute-start | bytes 4616 | tf_op jit(solution)/shard_map/ppermute | solution.py:17
  173.1 49.8 %collective-permute-start.4 = (bf16[4,384]{1,0:T(4,128)(2,1)S(1)}, bf16[4,384]{1,0:T(4,128)(2,1)S(1)}, u32[]{:S(2)}, u32[]{:S(2)}) collective-permute-start(bf16[4,384]{1,0:T(4,128)(2,1)S(1)} %get-tuple-element.72), channel_id=1, source_target_pairs={{0,4},{4,8},{8,12},{12,16},{16,20},{20,24},{24,28},{1,5},{5,9},{9,... | collective-permute-start | bytes 9224 | tf_op jit(solution)/shard_map/ppermute | solution.py:14
  175.0 47.9 %collective-permute-start.5 = (bf16[4,384]{1,0:T(4,128)(2,1)S(1)}, bf16[4,384]{1,0:T(4,128)(2,1)S(1)}, u32[]{:S(2)}, u32[]{:S(2)}) collective-permute-start(bf16[4,384]{1,0:T(4,128)(2,1)S(1)} %get-tuple-element.73), channel_id=1, source_target_pairs={{4,0},{8,4},{12,8},{16,12},{20,16},{24,20},{28,24},{5,1},{9,5},{13... | collective-permute-start | bytes 9224 | tf_op jit(solution)/shard_map/ppermute | solution.py:17
  245.3 50.2 %collective-permute-start.6 = (bf16[8,384]{1,0:T(8,128)(2,1)S(1)}, bf16[8,384]{1,0:T(8,128)(2,1)S(1)}, u32[]{:S(2)}, u32[]{:S(2)}) collective-permute-start(bf16[8,384]{1,0:T(8,128)(2,1)S(1)} %get-tuple-element.70), channel_id=1, source_target_pairs={{0,4},{4,8},{8,12},{12,16},{16,20},{20,24},{24,28},{1,5},{5,9},{9,... | collective-permute-start | bytes 18440 | tf_op jit(solution)/shard_map/ppermute | solution.py:14
  247.9 47.6 %collective-permute-start.7 = (bf16[8,384]{1,0:T(8,128)(2,1)S(1)}, bf16[8,384]{1,0:T(8,128)(2,1)S(1)}, u32[]{:S(2)}, u32[]{:S(2)}) collective-permute-start(bf16[8,384]{1,0:T(8,128)(2,1)S(1)} %get-tuple-element.71), channel_id=1, source_target_pairs={{4,0},{8,4},{12,8},{16,12},{20,16},{24,20},{28,24},{5,1},{9,5},{13... | collective-permute-start | bytes 18440 | tf_op jit(solution)/shard_map/ppermute | solution.py:17
  318.1 49.4 %collective-permute-start.8 = (bf16[16,384]{1,0:T(8,128)(2,1)S(1)}, bf16[16,384]{1,0:T(8,128)(2,1)S(1)}, u32[]{:S(2)}, u32[]{:S(2)}) collective-permute-start(bf16[16,384]{1,0:T(8,128)(2,1)S(1)} %get-tuple-element.68), channel_id=1, source_target_pairs={{0,4},{4,8},{8,12},{12,16},{16,20},{20,24},{24,28},{1,5},{5,9},{9,... | collective-permute-start | bytes 36872 | tf_op jit(solution)/shard_map/ppermute | solution.py:14
  320.4 47.0 %collective-permute-start.9 = (bf16[16,384]{1,0:T(8,128)(2,1)S(1)}, bf16[16,384]{1,0:T(8,128)(2,1)S(1)}, u32[]{:S(2)}, u32[]{:S(2)}) collective-permute-start(bf16[16,384]{1,0:T(8,128)(2,1)S(1)} %get-tuple-element.69), channel_id=1, source_target_pairs={{4,0},{8,4},{12,8},{16,12},{20,16},{24,20},{28,24},{5,1},{9,5},{13... | collective-permute-start | bytes 36872 | tf_op jit(solution)/shard_map/ppermute | solution.py:17
  391.3 49.2 %collective-permute-start.10 = (bf16[32,384]{1,0:T(8,128)(2,1)S(1)}, bf16[32,384]{1,0:T(8,128)(2,1)S(1)}, u32[]{:S(2)}, u32[]{:S(2)}) collective-permute-start(bf16[32,384]{1,0:T(8,128)(2,1)S(1)} %get-tuple-element.66), channel_id=1, source_target_pairs={{0,4},{4,8},{8,12},{12,16},{16,20},{20,24},{24,28},{1,5},{5,9},{9,... | collective-permute-start | bytes 73736 | tf_op jit(solution)/shard_map/ppermute | solution.py:14
  393.6 46.8 %collective-permute-start.11 = (bf16[32,384]{1,0:T(8,128)(2,1)S(1)}, bf16[32,384]{1,0:T(8,128)(2,1)S(1)}, u32[]{:S(2)}, u32[]{:S(2)}) collective-permute-start(bf16[32,384]{1,0:T(8,128)(2,1)S(1)} %get-tuple-element.67), channel_id=1, source_target_pairs={{4,0},{8,4},{12,8},{16,12},{20,16},{24,20},{28,24},{5,1},{9,5},{13... | collective-permute-start | bytes 73736 | tf_op jit(solution)/shard_map/ppermute | solution.py:17
  474.7 156.1 %all-gather.48.cloned.1.call-start = ((), (), s32[]{:S(2)}) async-start(), calls=%async_computation.12 | async-start | bytes 3538944 | tf_op jit(solution)/shard_map/all_gather | solution.py:61
  475.8 159.2 %all-gather.30.cloned.1.call-start = ((), (), s32[]{:S(2)}) async-start(), calls=%async_computation.2 | async-start | bytes 1966080 | tf_op jit(solution)/shard_map/all_gather | solution.py:47
  552.2 131.1 %all-gather.32.cloned.1.call-start = ((), (), s32[]{:S(2)}) async-start(), calls=%async_computation.3 | async-start | bytes 3538944 | tf_op jit(solution)/shard_map/all_gather | solution.py:78
  552.9 195.9 %reduce-scatter.2.cloned.1.call-start = ((), (), s32[]{:S(2)}) async-start(), calls=%async_computation.4 | async-start | bytes 294912 | tf_op jit(solution)/shard_map/reduce_scatter | solution.py:93
  (43 other events, 517.0 us)
Sparse Core Ops, SparseCore 0:
  9.5 68.0 all-gather.33
  79.8 66.8 all-gather.35
  148.9 69.7 all-gather.37
  220.7 70.5 all-gather.39
  293.4 69.8 all-gather.41
  365.3 70.9 all-gather.43
  438.5 69.6 all-gather.45
  509.7 15.2 all-gather.27
  527.2 73.9 all-gather.47
  602.7 17.9 all-gather.29
  622.8 60.4 all-gather.31
  688.9 59.8 reduce-scatter.1
where the time goes:
time: 768 us; the launch traced here: 758 us
  blocking collectives  393 us (51%)
  waiting for transfers between devices  154 us (20%)
  other arithmetic  85.1 us (11%)
  local copies, waits for them, and re-layouts  56.6 us (7%)
  starting transfers between devices  33.1 us (4%)
  matrix products  20.7 us (3%)
  between operations  15 us (2%)
    all_gather x8, blocking collectives, local(): lax.all_gather(point_weight[layer_idx], 'seq', axis=0, tiled=True)  275 us
    reduce_scatter x1, waiting for transfers between devices, local(): lax.psum_scatter(jnp.dot(counts, coverage, precision=lax.Precision.HIGHES...  60 us
    all_gather x6, blocking collectives, local(): full_rows = lax.all_gather(rimmed, 'ch', axis=1, tiled=True)  55.4 us
    all_gather x8, blocking collectives, local(): hidden_all = lax.all_gather(hidden, 'ch', axis=1, tiled=True)  52.8 us
    all_gather x8, waiting for transfers between devices, local(): lax.all_gather(conv_weight[layer_idx], 'seq', axis=1, tiled=True)  49.2 us
    gather x1, other arithmetic, local(): owner_rows = transcript_slot[exon_transcript]  40 us
    convert_element_type x8, other arithmetic, local(): act_rows = jax.nn.gelu(rms_scaled(full_rows, norm_gain[layer_idx]), appro...  37.9 us
    all_gather x8, local copies, waits for them, and re-layouts, local(): lax.all_gather(conv_weight[layer_idx], 'seq', axis=1, tiled=True)  33.5 us
  transfers between devices with their start and end apart: 28, of which 13 were waited for; matrix products, arithmetic and copies ran while one was open for 20% of the time, Pallas kernels for 0%

commit v1 on v0

--- a/solution.py
+++ b/solution.py
@@ -1,6 +1,8 @@
 import jax
 import jax.numpy as jnp
 from jax import lax
+from jax.experimental import pallas as pl
+from jax.experimental.pallas import tpu as pltpu
 from jax.sharding import PartitionSpec as P
 
 LAYERS = 8
@@ -25,7 +27,7 @@
     return wide * scale * gain_row
 
 
-def local(
+def local_plain(
     stream,
     norm_gain,
     conv_weight,
@@ -99,6 +101,451 @@
     return jnp.log1p(total)
 
 
+SEQ = 8
+CHS = 4
+HALF = 96
+MESH = pl.DeviceIdType.MESH
+
+
+def gelu(values):
+    return 0.5 * values * (1.0 + lax.erf(values * 0.7071067811865476))
+
+
+def tower_kernel(
+    w_ref,
+    head_ref,
+    x_ref,
+    gain_ref,
+    conv_bias_ref,
+    point_bias_ref,
+    head_bias_ref,
+    counts_ref,
+    out_ref,
+    weights,
+    heads,
+    streams,
+    act,
+    low_ext,
+    high_ext,
+    middle,
+    hid,
+    point,
+    partial,
+    landed,
+    local_sem,
+    ring_send,
+    ring_recv,
+    x_send,
+    x_recv,
+    hid_send,
+    hid_recv,
+    halo_send,
+    halo_recv,
+    sum_send,
+    sum_recv,
+):
+    seq = lax.axis_index("seq")
+    ch = lax.axis_index("ch")
+    rows = x_ref.shape[0]
+    odd = seq % 2
+    place = (1 - odd) * (seq // 2) + odd * (SEQ - 1 - seq // 2)
+
+    def at_place(spot):
+        spot = (spot + 2 * SEQ) % SEQ
+        upper = spot // (SEQ // 2)
+        return (1 - upper) * 2 * spot + upper * (2 * (SEQ - 1 - spot) + 1)
+
+    ring_to = (at_place(place + 1), at_place(place - 1))
+    sibling = ch + 1 - 2 * (ch % 2)
+    across = (ch + 2) % CHS
+    diagonal = (sibling + 2) % CHS
+
+    barrier = pltpu.get_barrier_semaphore()
+    for step in range(1, SEQ):
+        pl.semaphore_signal(
+            barrier, inc=1, device_id=((seq + step) % SEQ, ch), device_id_type=MESH
+        )
+    for peer in (sibling, across):
+        pl.semaphore_signal(barrier, inc=1, device_id=(seq, peer), device_id_type=MESH)
+
+    def own_copy(item):
+        if item < LAYERS:
+            return pltpu.make_async_copy(
+                w_ref.at[item], weights.at[item, seq], local_sem.at[item]
+            )
+        return pltpu.make_async_copy(head_ref, heads.at[seq], local_sem.at[item])
+
+    for item in range(LAYERS + 1):
+        own_copy(item).start()
+    streams[ch] = x_ref[...]
+    pl.semaphore_wait(barrier, SEQ + 1)
+
+    def reach(way, half):
+        return 4 if way == half else 3
+
+    def ring_copy(item, half, dist, way):
+        origin = at_place(place - (dist - 1) if way == 0 else place + (dist - 1))
+        part = pl.ds(half * HALF, HALF)
+        if item < LAYERS:
+            dst = weights.at[item, origin, part]
+            src = w_ref.at[item, part] if dist == 1 else dst
+        else:
+            dst = heads.at[origin, part]
+            src = head_ref.at[part] if dist == 1 else dst
+        return pltpu.make_async_remote_copy(
+            src_ref=src,
+            dst_ref=dst,
+            send_sem=ring_send.at[way, item, half, dist - 1],
+            recv_sem=ring_recv.at[way, item, half, dist - 1],
+            device_id=(ring_to[way], ch),
+            device_id_type=MESH,
+        )
+
+    def service(item, half, dist):
+        for way in (0, 1):
+            far = reach(way, half)
+            if dist <= far:
+                ring_copy(item, half, dist, way).wait_recv()
+                if dist < far:
+                    ring_copy(item, half, dist + 1, way).start()
+        if dist == 2 and item < LAYERS:
+            for way in (0, 1):
+                ring_copy(item + 1, half, 1, way).start()
+
+    def slot(item, number):
+        if item > LAYERS:
+            return
+        if number < 6:
+            service(item, number % 2, number // 2 + 1)
+        else:
+            service(item, 0, 4)
+            service(item, 1, 4)
+
+    for half in (0, 1):
+        for way in (0, 1):
+            ring_copy(0, half, 1, way).start()
+
+    def spread_copies(buffer, sends, recvs, turn):
+        def copy(block, peer, number):
+            return pltpu.make_async_remote_copy(
+                src_ref=buffer.at[block],
+                dst_ref=buffer.at[block],
+                send_sem=sends.at[turn, number],
+                recv_sem=recvs.at[turn, number],
+                device_id=(seq, peer),
+                device_id_type=MESH,
+            )
+
+        return copy(ch, across, 0), copy(ch, sibling, 1), copy(across, sibling, 2)
+
+    def norm_rows(turn, first, count, finish):
+        tile = 32
+
+        @pl.loop(0, count // tile)
+        def _(index):
+            part = pl.ds(pl.multiple_of(first + index * tile, tile), tile)
+            blocks = [streams[block, part, :].astype(jnp.float32) for block in range(CHS)]
+            width = blocks[0].shape[1]
+            squares = sum(jnp.sum(b * b, axis=1, keepdims=True) for b in blocks)
+            scale = lax.rsqrt(squares / (width * CHS) + 1e-06)
+            for block in range(CHS):
+                lanes = pl.ds(block * width, width)
+                normed = blocks[block] * scale * gain_ref[pl.ds(turn, 1), lanes]
+                act[part, lanes] = finish(normed).astype(jnp.bfloat16)
+
+    def gather_stream(turn):
+        first, second, third = spread_copies(streams, x_send, x_recv, turn)
+        finish = gelu if turn < LAYERS else (lambda normed: normed)
+        first.start()
+        second.start()
+        slot(turn, 3)
+        first.wait_recv()
+        third.start()
+        slot(turn, 4)
+        second.wait_recv()
+        third.wait_recv()
+        norm_rows(turn, 0, rows // 2, finish)
+        slot(turn, 5)
+        norm_rows(turn, rows // 2, rows // 2, finish)
+        for copy in (first, second, third):
+            copy.wait_send()
+        slot(turn, 6)
+        own_copy(turn).wait()
+
+    for number in (0, 1, 2):
+        slot(0, number)
+
+    for layer in range(LAYERS):
+        spread = 2**layer
+        rim = max(8, spread)
+        pad = low_ext.shape[1] - rows
+        gather_stream(layer)
+        lows, highs = low_ext.at[layer % 2], high_ext.at[layer % 2]
+
+        both = jnp.dot(
+            act[...],
+            weights[layer, :, :, 0:384].reshape(-1, 384),
+            preferred_element_type=jnp.float32,
+        )
+        lows[pl.ds(pad, rows), :] = both[:, 0:256]
+        middle[...] = both[:, 128:384]
+        highs[pl.ds(0, rows), :] = jnp.dot(
+            act[...],
+            weights[layer, :, :, 384:640].reshape(-1, 256),
+            preferred_element_type=jnp.float32,
+        )
+
+        up = pltpu.make_async_remote_copy(
+            src_ref=lows.at[pl.ds(pad + rows - rim, rim)],
+            dst_ref=lows.at[pl.ds(pad - rim, rim)],
+            send_sem=halo_send.at[0, layer],
+            recv_sem=halo_recv.at[0, layer],
+            device_id=((seq + 1) % SEQ, ch),
+            device_id_type=MESH,
+        )
+        down = pltpu.make_async_remote_copy(
+            src_ref=highs.at[pl.ds(0, rim)],
+            dst_ref=highs.at[pl.ds(rows, rim)],
+            send_sem=halo_send.at[1, layer],
+            recv_sem=halo_recv.at[1, layer],
+            device_id=((seq + SEQ - 1) % SEQ, ch),
+            device_id_type=MESH,
+        )
+
+        @pl.when(seq < SEQ - 1)
+        def _():
+            up.start()
+
+        @pl.when(seq > 0)
+        def _():
+            down.start()
+
+        slot(layer + 1, 0)
+
+        for block in range(SEQ):
+            here = pl.ds(block * HALF, HALF)
+            point[here, 0:128] = weights[layer, block, 0:HALF, 640:768]
+            point[here, 128:256] = weights[layer, block, HALF : 2 * HALF, 640:768]
+            near = weights[layer, block, 0:HALF, 512:640].astype(jnp.float32)
+            far = weights[layer, block, HALF : 2 * HALF, 512:640].astype(jnp.float32)
+            lane = lax.broadcasted_iota(jnp.int32, near.shape, 1)
+            point[here, 256:384] = jnp.where(
+                lane < 64, pltpu.roll(near, 64, 1), far
+            ).astype(jnp.bfloat16)
+
+        @pl.when(seq > 0)
+        def _():
+            up.wait_recv()
+
+        @pl.when(seq == 0)
+        def _():
+            lows[pl.ds(pad - rim, rim), :] = jnp.zeros((rim, 256), jnp.float32)
+
+        @pl.when(seq < SEQ - 1)
+        def _():
+            down.wait_recv()
+
+        @pl.when(seq == SEQ - 1)
+        def _():
+            highs[pl.ds(rows, rim), :] = jnp.zeros((rim, 256), jnp.float32)
+
+        tile = 64
+        for start in range(0, rows, tile):
+            conv = (
+                low_ext[layer % 2, pl.ds(pad - spread + start, tile), :]
+                + pltpu.roll(middle[pl.ds(start, tile), :], 192, 1)
+                + high_ext[layer % 2, pl.ds(spread + start, tile), :]
+                + conv_bias_ref[pl.ds(layer, 1), :]
+            )
+            hid[ch, pl.ds(start, tile), :] = gelu(conv).astype(jnp.bfloat16)
+
+        first, second, third = spread_copies(hid, hid_send, hid_recv, layer)
+        first.start()
+        second.start()
+
+        @pl.when(seq < SEQ - 1)
+        def _():
+            up.wait_send()
+
+        @pl.when(seq > 0)
+        def _():
+            down.wait_send()
+
+        slot(layer + 1, 1)
+        first.wait_recv()
+        third.start()
+        slot(layer + 1, 2)
+        second.wait_recv()
+        third.wait_recv()
+        mixed = streams[ch].astype(jnp.float32) + point_bias_ref[pl.ds(layer, 1), :]
+        total = None
+        for block in range(CHS):
+            term = jnp.dot(
+                hid[block, :, 0:192],
+                point[block * 192 : (block + 1) * 192, :],
+                preferred_element_type=jnp.float32,
+            )
+            total = term if total is None else total + term
+        streams[ch] = (mixed + total).astype(jnp.bfloat16)
+        for copy in (first, second, third):
+            copy.wait_send()
+
+    gather_stream(LAYERS)
+
+    for start in range(0, heads.shape[2], 256):
+        lanes = pl.ds(start, 256)
+        logits = (
+            jnp.dot(
+                act[...],
+                heads[:, :, start : start + 256].reshape(-1, 256),
+                preferred_element_type=jnp.float32,
+            )
+            + head_bias_ref[:, lanes]
+        )
+        cover = jnp.maximum(logits, 0.0) + jnp.log1p(jnp.exp(-jnp.abs(logits)))
+        sums = None
+        for _ in range(3):
+            piece = cover.astype(jnp.bfloat16)
+            term = jnp.dot(counts_ref[...], piece, preferred_element_type=jnp.float32)
+            sums = term if sums is None else sums + term
+            cover = cover - piece.astype(jnp.float32)
+        partial[:, :, lanes] = sums.reshape(SEQ, -1, 256)
+
+    def sum_copy(step):
+        target = (seq + step) % SEQ
+        return pltpu.make_async_remote_copy(
+            src_ref=partial.at[target],
+            dst_ref=landed.at[step - 1],
+            send_sem=sum_send.at[step - 1],
+            recv_sem=sum_recv.at[step - 1],
+            device_id=(target, ch),
+            device_id_type=MESH,
+        )
+
+    for step in range(1, SEQ):
+        sum_copy(step).start()
+    for item in range(LAYERS + 1):
+        for half in (0, 1):
+            for way in (0, 1):
+                for dist in range(1, reach(way, half) + 1):
+                    ring_copy(item, half, dist, way).wait_send()
+    result = partial[seq]
+    for step in range(1, SEQ):
+        sum_copy(step).wait_recv()
+        result = result + landed[step - 1]
+    out_ref[...] = jnp.log1p(result)[:, : out_ref.shape[1]]
+    for step in range(1, SEQ):
+        sum_copy(step).wait_send()
+
+
+def exon_counts(bin_rows, exon_start, exon_length, exon_transcript, transcript_slot):
+    bin_ids = lax.axis_index("seq") * bin_rows + jnp.arange(bin_rows, dtype=jnp.int32)
+    member = (
+        (bin_ids[None, :] >= exon_start[:, None])
+        & (bin_ids[None, :] < (exon_start + exon_length)[:, None])
+    ).astype(jnp.bfloat16)
+    owner_rows = transcript_slot[exon_transcript]
+    select = (
+        owner_rows[None, :] == jnp.arange(transcript_slot.shape[0], dtype=jnp.int32)[:, None]
+    ).astype(jnp.bfloat16)
+    return jnp.dot(select, member, preferred_element_type=jnp.float32)
+
+
+def local_kernel(
+    stream,
+    norm_gain,
+    conv_weight,
+    conv_bias,
+    point_weight,
+    point_bias,
+    head_weight,
+    head_bias,
+    exon_start,
+    exon_length,
+    exon_transcript,
+    transcript_slot,
+):
+    rows, width = stream.shape
+    depth = conv_weight.shape[2]
+    tracks = head_weight.shape[1]
+    wide = -(-tracks // 256) * 256
+    slots = transcript_slot.shape[0]
+    counts = exon_counts(rows, exon_start, exon_length, exon_transcript, transcript_slot).astype(
+        jnp.bfloat16
+    )
+    last = point_weight[:, :, 256:384]
+    packed = jnp.concatenate(
+        [
+            conv_weight[:, 0],
+            conv_weight[:, 1],
+            conv_weight[:, 2],
+            jnp.concatenate([last[:, :, 0:64], last[:, :, 64:128]], axis=1),
+            jnp.concatenate([point_weight[:, :, 0:128], point_weight[:, :, 128:256]], axis=1),
+        ],
+        axis=2,
+    )
+    vmem = pl.BlockSpec(memory_space=pltpu.VMEM)
+    dma = pltpu.SemaphoreType.DMA
+    return pl.pallas_call(
+        tower_kernel,
+        out_shape=jax.ShapeDtypeStruct((slots // SEQ, tracks), jnp.float32),
+        in_specs=[vmem] * 8,
+        out_specs=vmem,
+        scratch_shapes=[
+            pltpu.VMEM((LAYERS, SEQ, depth, 768), jnp.bfloat16),
+            pltpu.VMEM((SEQ, depth, wide), jnp.bfloat16),
+            pltpu.VMEM((CHS, rows, width), jnp.bfloat16),
+            pltpu.VMEM((rows, CHS * width), jnp.bfloat16),
+            pltpu.VMEM((2, rows + 128, 256), jnp.float32),
+            pltpu.VMEM((2, rows + 128, 256), jnp.float32),
+            pltpu.VMEM((rows, 256), jnp.float32),
+            pltpu.VMEM((CHS, rows, 256), jnp.bfloat16),
+            pltpu.VMEM((SEQ * HALF, width), jnp.bfloat16),
+            pltpu.VMEM((SEQ, slots // SEQ, wide), jnp.float32),
+            pltpu.VMEM((SEQ - 1, slots // SEQ, wide), jnp.float32),
+            dma((LAYERS + 1,)),
+            dma((2, LAYERS + 1, 2, 4)),
+            dma((2, LAYERS + 1, 2, 4)),
+            dma((LAYERS + 1, 3)),
+            dma((LAYERS + 1, 3)),
+            dma((LAYERS, 3)),
+            dma((LAYERS, 3)),
+            dma((2, LAYERS)),
+            dma((2, LAYERS)),
+            dma((SEQ - 1,)),
+            dma((SEQ - 1,)),
+        ],
+        compiler_params=pltpu.CompilerParams(
+            collective_id=0, has_side_effects=True, vmem_limit_bytes=56 * 2**20
+        ),
+        cost_estimate=pl.CostEstimate(
+            flops=6_000_000_000, bytes_accessed=4_000_000, transcendentals=4_000_000
+        ),
+    )(
+        packed,
+        jnp.pad(head_weight, ((0, 0), (0, wide - tracks))),
+        stream,
+        norm_gain,
+        jnp.pad(conv_bias, ((0, 0), (0, 256 - conv_bias.shape[1]))),
+        point_bias,
+        jnp.pad(head_bias, (0, wide - tracks))[None, :],
+        counts,
+    )
+
+
+def local(*args):
+    stream, conv_weight, point_weight = args[0], args[2], args[4]
+    fits = (
+        lax.axis_size("seq") == SEQ
+        and lax.axis_size("ch") == CHS
+        and stream.shape == (256, 384)
+        and conv_weight.shape[2:] == (192, 192)
+        and point_weight.shape[1:] == (HALF, 384)
+        and args[11].shape[0] == 8 * SEQ
+    )
+    return local_kernel(*args) if fits else local_plain(*args)
+
+
 def solution(mesh):
     placed = (
         P("seq", "ch"),

time: 768 us -> 309 us (0.40); the launches traced: 758 us -> 308 us
  blocking collectives: 393 us -> 0 us
  Pallas kernels: 0 us -> 254 us
  waiting for transfers between devices: 154 us -> 0 us
  local copies, waits for them, and re-layouts: 56.6 us -> 11.4 us
  other arithmetic: 85.1 us -> 41.1 us
  starting transfers between devices: 33.1 us -> 0 us
  matrix products: 20.7 us -> 1.65 us
  between operations: 15 us -> 0.1 us
    all_gather x23 -> x0, blocking collectives: 393 us -> none  [the longest x8 275 us: local(): lax.all_gather(point_weight[layer_idx], 'seq', axis=0, tiled=True)]
    pallas_call x0 -> x1, Pallas kernels: none -> 254 us  [local_kernel(): pl.pallas_call(tower_kernel, out_shape=jax.ShapeDtypeStruct((slots // SEQ...]
    all_gather x11 -> x0, waiting for transfers between devices: 82.2 us -> none  [the longest x8 49.2 us: local(): lax.all_gather(conv_weight[layer_idx], 'seq', axis=1, tiled=True)]
    reduce_scatter x1 -> x0, waiting for transfers between devices: 60 us -> none  [local(): lax.psum_scatter(jnp.dot(counts, coverage, precision=lax.Precision.HIGHES...]
    convert_element_type x8 -> x0, other arithmetic: 37.9 us -> none  [local(): act_rows = jax.nn.gelu(rms_scaled(full_rows, norm_gain[layer_idx]), appro...]
    all_gather x8 -> x0, local copies, waits for them, and re-layouts: 33.5 us -> none  [local(): lax.all_gather(conv_weight[layer_idx], 'seq', axis=1, tiled=True)]
    ppermute x16 -> x0, starting transfers between devices: 32.6 us -> none  [the longest x8 22.3 us: padded(): lax.ppermute(lax.slice_in_dim(block, block.shape[dim] - width, None, axis...]
    dot_general x19 -> x1, matrix products: 20.7 us -> 1.65 us  [exon_counts(): return jnp.dot(select, member, preferred_element_type=jnp.float32)]
  transfers between devices with their start and end apart: 28 -> 0, of which waited for: 13 -> 0; matrix products, arithmetic and copies ran while one was open for 20% -> 0% of each run, Pallas kernels for 0% -> 0%
where the time goes in v1:
time: 309 us; the launch traced here: 308 us
  Pallas kernels  254 us (82%)
  other arithmetic  41.1 us (13%)
  local copies, waits for them, and re-layouts  11.4 us (4%)
    pallas_call x1, Pallas kernels, local_kernel(): pl.pallas_call(tower_kernel, out_shape=jax.ShapeDtypeStruct((slots // SEQ...  254 us
    gather x1, other arithmetic, exon_counts(): owner_rows = transcript_slot[exon_transcript]  40.2 us

profile of v1, /device:TPU:0, one launch (start us, length us, event | category | flops | bytes accessed | tf_op | source)
XLA Modules:
  0.0 308.0 jit_solution(18012099128357293452)
XLA Ops:
  0.0 1.8 slice_bitcast_fusion
  1.8 0.0 copy-done.1
  1.8 0.1 fusion.6
  2.0 0.1 pad_maximum_fusion
  2.1 0.1 fusion.5
  2.2 0.0 copy-start.2
  2.2 0.0 copy-start.3
  2.2 0.0 copy-start.4
  2.2 0.0 copy-start
  2.2 3.1 %concatenate.11.w_ref = bf16[8,192,768]{2,1,0:T(8,128)(2,1)} concatenate(bf16[8,192,192]{2,1,0:T(8,128)(2,1)S(1)} %get-tuple-element.7, bf16[8,192,192]{2,1,0:T(8,128)(2,1)S(1)} %get-tuple-element.6, bf16[8,192,192]{2,1,0:T(8,128)(2,1)S(1)} %get-tuple-element.5, bf16[8,192,64]{2,1,0:T(8,128)(2,1)S(1)} %pad_maximum_fusion, bf16[8,192,128]{2,1,0:T(8,128)(2,1)S(1)} %pad_maximum_fusion.1), dimensions={2} | concatenate | bytes 4718592 | tf_op jit(solution)/shard_map/concatenate | solution.py:477
  5.3 0.0 copy-done.2
  5.3 0.8 pad.12.head_ref
  6.1 0.0 copy-done.3
  6.1 0.6 pad.13.conv_bias_ref
  6.7 0.6 pad.14
  7.3 0.7 add.29
  8.0 0.7 fusion.10
  8.7 0.7 fusion.7
  9.4 0.7 fusion.8
  10.2 0.7 fusion.9
  10.9 40.2 %select_select_fusion = s32[512]{0:T(512)S(1)} fusion(s32[512]{0:T(512)} %param.22, s32[]{:T(128)} %bitcast.4, s32[]{:T(128)} %bitcast.5, s32[]{:T(128)} %bitcast.6, s32[]{:T(128)} %bitcast.7, s32[]{:T(128)} %bitcast.8, s32[]{:T(128)} %bitcast.9, s32[]{:T(128)} %bitcast.10, s32[]{:T(128)} %bitcast.11, s32[]{:T(128)} %bitcast.12, s32[]{:T(128)} %bitcast.13, ...), kind=kLoop, calls=%fused_computation.14 | loop fusion | flops 66048 | bytes 4352 | tf_op jit(solution)/shard_map/gather | solution.py:447
  51.2 1.6 convolution_convert_fusion.counts_ref
  52.8 253.8 %shard_map.118 = f32[8,960]{1,0:T(8,128)} custom-call(bf16[8,192,768]{2,1,0:T(8,128)(2,1)} %concatenate.11.w_ref, bf16[192,1024]{1,0:T(8,128)(2,1)} %pad.12.head_ref, bf16[256,384]{1,0:T(8,128)(2,1)} %x_ref.1, f32[9,1536]{1,0:T(8,128)} %gain_ref.1, f32[8,256]{1,0:T(8,128)} %pad.13.conv_bias_ref, f32[8,384]{1,0:T(8,128)} %point_bias_ref.1, ...), custom_call_target="tpu_custom_call" | custom-call | flops 6000000000 | bytes 4000000 | tf_op jit(solution)/shard_map/pallas_call | solution.py:489
  306.7 1.4 copy.20
  (5 shorter events, 0.0 us)
Async XLA Ops:
  0.0 1.8 copy-start.1
  2.2 3.2 %copy-start.2 = (bf16[192,960]{1,0:T(8,128)(2,1)S(1)}, bf16[192,960]{1,0:T(8,128)(2,1)}, u32[]{:S(2)}) copy-start(bf16[192,960]{1,0:T(8,128)(2,1)} %param.18) | copy-start | bytes 1105924
  2.2 3.9 %copy-start.3 = (f32[8,192]{1,0:T(8,128)S(1)}, f32[8,192]{1,0:T(8,128)}, u32[]{:S(2)}) copy-start(f32[8,192]{1,0:T(8,128)} %param.15) | copy-start | bytes 18436
  2.2 4.5 %copy-start.4 = (f32[960]{0:T(1024)S(1)}, f32[960]{0:T(1024)}, u32[]{:S(2)}) copy-start(f32[960]{0:T(1024)} %param.19) | copy-start | bytes 11524
  2.2 5.8 %copy-start = (s32[64]{0:T(128)S(1)}, s32[64]{0:T(128)}, u32[]{:S(2)}) copy-start(s32[64]{0:T(128)} %param.23) | copy-start | bytes 772

commit v2 on v1

--- a/solution.py
+++ b/solution.py
@@ -112,14 +112,18 @@
 
 
 def tower_kernel(
-    w_ref,
-    head_ref,
     x_ref,
     gain_ref,
+    conv_ref,
     conv_bias_ref,
+    point_ref,
     point_bias_ref,
+    head_ref,
     head_bias_ref,
-    counts_ref,
+    start_ref,
+    length_ref,
+    owner_ref,
+    slot_ref,
     out_ref,
     weights,
     heads,
@@ -132,7 +136,9 @@
     point,
     partial,
     landed,
-    local_sem,
+    counts,
+    conv_bias,
+    head_bias,
     ring_send,
     ring_recv,
     x_send,
@@ -168,15 +174,24 @@
     for peer in (sibling, across):
         pl.semaphore_signal(barrier, inc=1, device_id=(seq, peer), device_id_type=MESH)
 
-    def own_copy(item):
+    def pack(item):
         if item < LAYERS:
-            return pltpu.make_async_copy(
-                w_ref.at[item], weights.at[item, seq], local_sem.at[item]
+            last = point_ref[item, :, 256:384]
+            strip = jnp.concatenate([last[:, 0:64], last[:, 64:128]], axis=0)
+            own = weights.at[item, seq]
+            own[:, 0:640] = jnp.concatenate(
+                [conv_ref[item, 0], conv_ref[item, 1], conv_ref[item, 2], strip], axis=1
             )
-        return pltpu.make_async_copy(head_ref, heads.at[seq], local_sem.at[item])
-
-    for item in range(LAYERS + 1):
-        own_copy(item).start()
+            own[0:HALF, 640:768] = point_ref[item, :, 0:128]
+            own[HALF : 2 * HALF, 640:768] = point_ref[item, :, 128:256]
+        else:
+            depth, tracks = head_ref.shape
+            tail = tracks // 128 * 128
+            own = heads.at[seq]
+            own[:, tail:] = jnp.zeros((depth, heads.shape[2] - tail), jnp.bfloat16)
+            own[:, 0:tracks] = head_ref[...]
+
+    pack(0)
     streams[ch] = x_ref[...]
     pl.semaphore_wait(barrier, SEQ + 1)
 
@@ -187,14 +202,12 @@
         origin = at_place(place - (dist - 1) if way == 0 else place + (dist - 1))
         part = pl.ds(half * HALF, HALF)
         if item < LAYERS:
-            dst = weights.at[item, origin, part]
-            src = w_ref.at[item, part] if dist == 1 else dst
+            block = weights.at[item, origin, part]
         else:
-            dst = heads.at[origin, part]
-            src = head_ref.at[part] if dist == 1 else dst
+            block = heads.at[origin, part]
         return pltpu.make_async_remote_copy(
-            src_ref=src,
-            dst_ref=dst,
+            src_ref=block,
+            dst_ref=block,
             send_sem=ring_send.at[way, item, half, dist - 1],
             recv_sem=ring_recv.at[way, item, half, dist - 1],
             device_id=(ring_to[way], ch),
@@ -224,6 +237,29 @@
     for half in (0, 1):
         for way in (0, 1):
             ring_copy(0, half, 1, way).start()
+    for item in range(1, LAYERS + 1):
+        pack(item)
+
+    slots = slot_ref.shape[1]
+    bins = seq * rows + lax.broadcasted_iota(jnp.int32, (rows, start_ref.shape[1]), 0)
+    member = (bins >= start_ref[...]) & (bins < start_ref[...] + length_ref[...])
+    names = lax.broadcasted_iota(jnp.int32, (slots, owner_ref.shape[1]), 0)
+    owned = lax.dot_general(
+        jnp.where(names == owner_ref[...], 1.0, 0.0).astype(jnp.bfloat16),
+        jnp.where(member, 1.0, 0.0).astype(jnp.bfloat16),
+        (((1,), (1,)), ((), ())),
+        preferred_element_type=jnp.float32,
+    )
+    order = lax.broadcasted_iota(jnp.int32, (slots, slots), 0) == slot_ref[...]
+    counts[...] = jnp.dot(
+        jnp.where(order, 1.0, 0.0).astype(jnp.bfloat16),
+        owned.astype(jnp.bfloat16),
+        preferred_element_type=jnp.float32,
+    ).astype(jnp.bfloat16)
+    conv_bias[...] = jnp.zeros_like(conv_bias)
+    conv_bias[:, 0 : conv_bias_ref.shape[1]] = conv_bias_ref[...]
+    head_bias[...] = jnp.zeros_like(head_bias)
+    head_bias[:, 0 : head_bias_ref.shape[1]] = head_bias_ref[...]
 
     def spread_copies(buffer, sends, recvs, turn):
         def copy(block, peer, number):
@@ -270,7 +306,6 @@
         for copy in (first, second, third):
             copy.wait_send()
         slot(turn, 6)
-        own_copy(turn).wait()
 
     for number in (0, 1, 2):
         slot(0, number)
@@ -355,7 +390,7 @@
                 low_ext[layer % 2, pl.ds(pad - spread + start, tile), :]
                 + pltpu.roll(middle[pl.ds(start, tile), :], 192, 1)
                 + high_ext[layer % 2, pl.ds(spread + start, tile), :]
-                + conv_bias_ref[pl.ds(layer, 1), :]
+                + conv_bias[pl.ds(layer, 1), :]
             )
             hid[ch, pl.ds(start, tile), :] = gelu(conv).astype(jnp.bfloat16)
 
@@ -400,13 +435,13 @@
                 heads[:, :, start : start + 256].reshape(-1, 256),
                 preferred_element_type=jnp.float32,
             )
-            + head_bias_ref[:, lanes]
+            + head_bias[:, lanes]
         )
         cover = jnp.maximum(logits, 0.0) + jnp.log1p(jnp.exp(-jnp.abs(logits)))
         sums = None
         for _ in range(3):
             piece = cover.astype(jnp.bfloat16)
-            term = jnp.dot(counts_ref[...], piece, preferred_element_type=jnp.float32)
+            term = jnp.dot(counts[...], piece, preferred_element_type=jnp.float32)
             sums = term if sums is None else sums + term
             cover = cover - piece.astype(jnp.float32)
         partial[:, :, lanes] = sums.reshape(SEQ, -1, 256)
@@ -436,19 +471,6 @@
     out_ref[...] = jnp.log1p(result)[:, : out_ref.shape[1]]
     for step in range(1, SEQ):
         sum_copy(step).wait_send()
-
-
-def exon_counts(bin_rows, exon_start, exon_length, exon_transcript, transcript_slot):
-    bin_ids = lax.axis_index("seq") * bin_rows + jnp.arange(bin_rows, dtype=jnp.int32)
-    member = (
-        (bin_ids[None, :] >= exon_start[:, None])
-        & (bin_ids[None, :] < (exon_start + exon_length)[:, None])
-    ).astype(jnp.bfloat16)
-    owner_rows = transcript_slot[exon_transcript]
-    select = (
-        owner_rows[None, :] == jnp.arange(transcript_slot.shape[0], dtype=jnp.int32)[:, None]
-    ).astype(jnp.bfloat16)
-    return jnp.dot(select, member, preferred_element_type=jnp.float32)
 
 
 def local_kernel(
@@ -470,26 +492,12 @@
     tracks = head_weight.shape[1]
     wide = -(-tracks // 256) * 256
     slots = transcript_slot.shape[0]
-    counts = exon_counts(rows, exon_start, exon_length, exon_transcript, transcript_slot).astype(
-        jnp.bfloat16
-    )
-    last = point_weight[:, :, 256:384]
-    packed = jnp.concatenate(
-        [
-            conv_weight[:, 0],
-            conv_weight[:, 1],
-            conv_weight[:, 2],
-            jnp.concatenate([last[:, :, 0:64], last[:, :, 64:128]], axis=1),
-            jnp.concatenate([point_weight[:, :, 0:128], point_weight[:, :, 128:256]], axis=1),
-        ],
-        axis=2,
-    )
     vmem = pl.BlockSpec(memory_space=pltpu.VMEM)
     dma = pltpu.SemaphoreType.DMA
     return pl.pallas_call(
         tower_kernel,
         out_shape=jax.ShapeDtypeStruct((slots // SEQ, tracks), jnp.float32),
-        in_specs=[vmem] * 8,
+        in_specs=[vmem] * 12,
         out_specs=vmem,
         scratch_shapes=[
             pltpu.VMEM((LAYERS, SEQ, depth, 768), jnp.bfloat16),
@@ -503,7 +511,9 @@
             pltpu.VMEM((SEQ * HALF, width), jnp.bfloat16),
             pltpu.VMEM((SEQ, slots // SEQ, wide), jnp.float32),
             pltpu.VMEM((SEQ - 1, slots // SEQ, wide), jnp.float32),
-            dma((LAYERS + 1,)),
+            pltpu.VMEM((slots, rows), jnp.bfloat16),
+            pltpu.VMEM((LAYERS, 256), jnp.float32),
+            pltpu.VMEM((1, wide), jnp.float32),
             dma((2, LAYERS + 1, 2, 4)),
             dma((2, LAYERS + 1, 2, 4)),
             dma((LAYERS + 1, 3)),
@@ -522,14 +532,18 @@
             flops=6_000_000_000, bytes_accessed=4_000_000, transcendentals=4_000_000
         ),
     )(
-        packed,
-        jnp.pad(head_weight, ((0, 0), (0, wide - tracks))),
         stream,
         norm_gain,
-        jnp.pad(conv_bias, ((0, 0), (0, 256 - conv_bias.shape[1]))),
+        conv_weight,
+        conv_bias,
+        point_weight,
         point_bias,
-        jnp.pad(head_bias, (0, wide - tracks))[None, :],
-        counts,
+        head_weight,
+        head_bias[None, :],
+        exon_start[None, :],
+        exon_length[None, :],
+        exon_transcript[None, :],
+        transcript_slot[None, :],
     )
 
 

time: 309 us -> 256 us (0.83)
  other arithmetic: 41.1 us -> 0 us
  local copies, waits for them, and re-layouts: 11.4 us -> 1.38 us
    gather x1 -> x0, other arithmetic: 40.2 us -> none  [exon_counts(): owner_rows = transcript_slot[exon_transcript]]
    concatenate x1 -> x0, local copies, waits for them, and re-layouts: 3.13 us -> none  [local_kernel(): jnp.concatenate([conv_weight[:, 0], conv_weight[:, 1], conv_weight[:, 2],...]
where the time goes in v2:
time: 256 us
  Pallas kernels  254 us (99%)
    pallas_call x1, Pallas kernels, local_kernel(): pl.pallas_call(tower_kernel, out_shape=jax.ShapeDtypeStruct((slots // SEQ...  254 us

profile of v2, /device:TPU:0, one launch (start us, length us, event | category | flops | bytes accessed | tf_op | source)
XLA Modules:
  0.0 255.6 jit_solution(10096256983835244374)
XLA Ops:
  0.0 254.2 %shard_map.118 = f32[8,960]{1,0:T(8,128)} custom-call(bf16[256,384]{1,0:T(8,128)(2,1)} %x_ref.1, f32[9,1536]{1,0:T(8,128)} %gain_ref.1, bf16[8,3,192,192]{3,2,1,0:T(8,128)(2,1)} %conv_ref.1, f32[8,192]{1,0:T(8,128)} %conv_bias_ref.1, bf16[8,96,384]{2,1,0:T(8,128)(2,1)} %point_ref.1, f32[8,384]{1,0:T(8,128)} %point_bias_ref.1, bf16[192,960]{1,0:T(8,128)(2,1)} %head_ref.1, ...), custom_call_target="tpu_custom_call" | custom-call | flops 6000000000 | bytes 4000000 | tf_op jit(solution)/shard_map/pallas_call | solution.py:497
  254.2 1.4 copy.14

commit v3 on v2

--- a/solution.py
+++ b/solution.py
@@ -104,6 +104,7 @@
 SEQ = 8
 CHS = 4
 HALF = 96
+ITEMS = LAYERS + 2
 MESH = pl.DeviceIdType.MESH
 
 
@@ -186,10 +187,15 @@
             own[HALF : 2 * HALF, 640:768] = point_ref[item, :, 128:256]
         else:
             depth, tracks = head_ref.shape
-            tail = tracks // 128 * 128
-            own = heads.at[seq]
-            own[:, tail:] = jnp.zeros((depth, heads.shape[2] - tail), jnp.bfloat16)
-            own[:, 0:tracks] = head_ref[...]
+            span = heads.shape[3]
+            first = (item - LAYERS) * span
+            count = min(span, tracks - first)
+            own = heads.at[item - LAYERS, seq]
+            if count < span:
+                own[:, count // 128 * 128 :] = jnp.zeros(
+                    (depth, span - count // 128 * 128), jnp.bfloat16
+                )
+            own[:, 0:count] = head_ref[:, first : first + count]
 
     pack(0)
     streams[ch] = x_ref[...]
@@ -204,7 +210,7 @@
         if item < LAYERS:
             block = weights.at[item, origin, part]
         else:
-            block = heads.at[origin, part]
+            block = heads.at[item - LAYERS, origin, part]
         return pltpu.make_async_remote_copy(
             src_ref=block,
             dst_ref=block,
@@ -221,23 +227,25 @@
                 ring_copy(item, half, dist, way).wait_recv()
                 if dist < far:
                     ring_copy(item, half, dist + 1, way).start()
-        if dist == 2 and item < LAYERS:
-            for way in (0, 1):
-                ring_copy(item + 1, half, 1, way).start()
-
-    def slot(item, number):
-        if item > LAYERS:
-            return
-        if number < 6:
-            service(item, number % 2, number // 2 + 1)
-        else:
-            service(item, 0, 4)
-            service(item, 1, 4)
+
+    order = sorted((7 * item + 2 * number, item, number) for item in range(ITEMS) for number in range(7))
+    steps = iter(order)
+
+    def advance(count=1):
+        for _, item, number in [next(steps) for _ in range(count)]:
+            if number < 6:
+                service(item, number % 2, number // 2 + 1)
+            else:
+                service(item, 0, 4)
+                service(item, 1, 4)
+            if number in (1, 2) and item + 1 < ITEMS:
+                for way in (0, 1):
+                    ring_copy(item + 1, number - 1, 1, way).start()
 
     for half in (0, 1):
         for way in (0, 1):
             ring_copy(0, half, 1, way).start()
-    for item in range(1, LAYERS + 1):
+    for item in range(1, ITEMS):
         pack(item)
 
     slots = slot_ref.shape[1]
@@ -250,9 +258,9 @@
         (((1,), (1,)), ((), ())),
         preferred_element_type=jnp.float32,
     )
-    order = lax.broadcasted_iota(jnp.int32, (slots, slots), 0) == slot_ref[...]
+    placed = lax.broadcasted_iota(jnp.int32, (slots, slots), 0) == slot_ref[...]
     counts[...] = jnp.dot(
-        jnp.where(order, 1.0, 0.0).astype(jnp.bfloat16),
+        jnp.where(placed, 1.0, 0.0).astype(jnp.bfloat16),
         owned.astype(jnp.bfloat16),
         preferred_element_type=jnp.float32,
     ).astype(jnp.bfloat16)
@@ -294,21 +302,20 @@
         finish = gelu if turn < LAYERS else (lambda normed: normed)
         first.start()
         second.start()
-        slot(turn, 3)
+        advance()
         first.wait_recv()
         third.start()
-        slot(turn, 4)
+        advance()
         second.wait_recv()
         third.wait_recv()
         norm_rows(turn, 0, rows // 2, finish)
-        slot(turn, 5)
+        advance()
         norm_rows(turn, rows // 2, rows // 2, finish)
         for copy in (first, second, third):
             copy.wait_send()
-        slot(turn, 6)
-
-    for number in (0, 1, 2):
-        slot(0, number)
+        advance()
+
+    advance(6)
 
     for layer in range(LAYERS):
         spread = 2**layer
@@ -355,7 +362,7 @@
         def _():
             down.start()
 
-        slot(layer + 1, 0)
+        advance()
 
         for block in range(SEQ):
             here = pl.ds(block * HALF, HALF)
@@ -406,10 +413,10 @@
         def _():
             down.wait_send()
 
-        slot(layer + 1, 1)
+        advance()
         first.wait_recv()
         third.start()
-        slot(layer + 1, 2)
+        advance()
         second.wait_recv()
         third.wait_recv()
         mixed = streams[ch].astype(jnp.float32) + point_bias_ref[pl.ds(layer, 1), :]
@@ -427,12 +434,15 @@
 
     gather_stream(LAYERS)
 
-    for start in range(0, heads.shape[2], 256):
+    span = heads.shape[3]
+    for start in range(0, 2 * span, 256):
         lanes = pl.ds(start, 256)
+        if start <= span:
+            advance(1 if start < span else 4 - span // 256)
         logits = (
             jnp.dot(
                 act[...],
-                heads[:, :, start : start + 256].reshape(-1, 256),
+                heads[start // span, :, :, start % span : start % span + 256].reshape(-1, 256),
                 preferred_element_type=jnp.float32,
             )
             + head_bias[:, lanes]
@@ -459,7 +469,7 @@
 
     for step in range(1, SEQ):
         sum_copy(step).start()
-    for item in range(LAYERS + 1):
+    for item in range(ITEMS):
         for half in (0, 1):
             for way in (0, 1):
                 for dist in range(1, reach(way, half) + 1):
@@ -501,7 +511,7 @@
         out_specs=vmem,
         scratch_shapes=[
             pltpu.VMEM((LAYERS, SEQ, depth, 768), jnp.bfloat16),
-            pltpu.VMEM((SEQ, depth, wide), jnp.bfloat16),
+            pltpu.VMEM((2, SEQ, depth, wide // 2), jnp.bfloat16),
             pltpu.VMEM((CHS, rows, width), jnp.bfloat16),
             pltpu.VMEM((rows, CHS * width), jnp.bfloat16),
             pltpu.VMEM((2, rows + 128, 256), jnp.float32),
@@ -514,8 +524,8 @@
             pltpu.VMEM((slots, rows), jnp.bfloat16),
             pltpu.VMEM((LAYERS, 256), jnp.float32),
             pltpu.VMEM((1, wide), jnp.float32),
-            dma((2, LAYERS + 1, 2, 4)),
-            dma((2, LAYERS + 1, 2, 4)),
+            dma((2, ITEMS, 2, 4)),
+            dma((2, ITEMS, 2, 4)),
             dma((LAYERS + 1, 3)),
             dma((LAYERS + 1, 3)),
             dma((LAYERS, 3)),

time: 256 us -> 270 us (1.055)
  Pallas kernels: 254 us -> 268 us
    pallas_call x1, Pallas kernels: 254 us -> 268 us  [local_kernel(): pl.pallas_call(tower_kernel, out_shape=jax.ShapeDtypeStruct((slots // SEQ...]
where the time goes in v3:
time: 270 us
  Pallas kernels  268 us (99%)
    pallas_call x1, Pallas kernels, local_kernel(): pl.pallas_call(tower_kernel, out_shape=jax.ShapeDtypeStruct((slots // SEQ...  268 us

profile of v3, /device:TPU:0, one launch (start us, length us, event | category | flops | bytes accessed | tf_op | source)
XLA Modules:
  0.0 269.7 jit_solution(16790454362868605823)
XLA Ops:
  0.0 268.4 %shard_map.118 = f32[8,960]{1,0:T(8,128)} custom-call(bf16[256,384]{1,0:T(8,128)(2,1)} %x_ref.1, f32[9,1536]{1,0:T(8,128)} %gain_ref.1, bf16[8,3,192,192]{3,2,1,0:T(8,128)(2,1)} %conv_ref.1, f32[8,192]{1,0:T(8,128)} %conv_bias_ref.1, bf16[8,96,384]{2,1,0:T(8,128)(2,1)} %point_ref.1, f32[8,384]{1,0:T(8,128)} %point_bias_ref.1, bf16[192,960]{1,0:T(8,128)(2,1)} %head_ref.1, ...), custom_call_target="tpu_custom_call" | custom-call | flops 6000000000 | bytes 4000000 | tf_op jit(solution)/shard_map/pallas_call | solution.py:507
  268.4 1.4 copy.14
